TPU v7x, 128 devices: a whole 4x4x4 slice. The times are simulated.
128 devices in a mesh: prow: 8 (over x, core), pcol: 16 (over y, z).
Axes of the slice: x: 4, y: 4, z: 4, core: 2. Of those that a mesh axis runs over, the one named last changes fastest.
Arguments:
- front: float32 [59, 8, 128, 1, 16, 128], P(None, 'prow', None, None, 'pcol'), may hold values from -66 to 396
- child: float32 [2, 8, 8, 128, 16, 128], P(None, None, 'prow', None, 'pcol'), may hold values from -6 to 6
- row_map: int32 [2, 64], replicated, may hold values from 0 to 471, as said below
- col_map: int32 [2, 16], replicated, may hold values from 0 to 15, as said below
Outputs:
- factor: float32 [59, 8, 128, 1, 16, 128], P(None, 'prow', None, None, 'pcol')
Inputs may be any that keep to these rules, and one draw needn't show every extreme that they name: Within one child all entries differ. For each child c and each index p of prow, the entries row_map[c, l * 8 + p] for l = 0 .. 7 have different remainders modulo 8. `col_map`: within one child all entries differ.
All inputs are finite; a program needn't handle non-finite values.
Results may differ from a plain program's by a relative error of at most 0.0001.
Values sent between devices are 32-bit elements; how exact they have to be, the bound alone decides.
No kernel may reach another device: no remote copies, remote signals or barrier semaphores. Data moves between devices by JAX's collectives and lax.ppermute only.
A program may use at most 128 MiB of HBM per device.

v0:
```python
import jax
import jax.numpy as jnp
from jax import lax
from jax.sharding import PartitionSpec as P

HIGHEST_PRECISION = lax.Precision.HIGHEST


def broadcast(block, axis, holder):
    block = jnp.where(lax.axis_index(axis) == holder, block, jnp.zeros_like(block))
    return lax.psum(block, axis)


def spread(strip, root):
    return broadcast(strip, "pcol", root)


def sort_by_owner(blocks, owners, prow_count):
    choose = (owners[:, None, :] == jnp.arange(prow_count)[None, :, None]).astype(jnp.float32)
    return jnp.einsum("cdl,clrx->cdrx", choose, blocks, precision=HIGHEST_PRECISION)


def place_columns(carry, piece, col_map, col_here, pcol_count, block_size):
    count = piece.shape[3] // block_size
    target = jnp.arange(carry.shape[3]) * pcol_count + col_here
    pick = (col_map[:, :, None] == target[None, None, :]).astype(jnp.float32)
    shaped = piece.reshape(piece.shape[0], piece.shape[1], block_size, count, block_size)
    return jnp.einsum("csrtk,ctm->csrmk", shaped, pick, precision=HIGHEST_PRECISION)


def on_device(front, child, row_map, col_map):
    row_blocks = front.shape[0]
    block_size = front.shape[2]
    col_blocks = front.shape[3]
    prow_count = lax.axis_size("prow")
    pcol_count = lax.axis_size("pcol")
    row_here = lax.axis_index("prow")
    col_here = lax.axis_index("pcol")
    local_rows = child.shape[1]
    matrix = front.reshape(row_blocks * block_size, col_blocks * block_size)
    table = row_map.reshape(2, local_rows, prow_count)
    owners = (
        jnp.sum(jnp.where(jnp.arange(prow_count)[None, None, :] == row_here, table, 0), axis=2)
        % prow_count
    )
    arrival = jnp.sum(jnp.where(table % prow_count == row_here, table // prow_count, 0), axis=1)
    raw = child.reshape(2, local_rows, block_size, block_size)
    moved = lax.all_to_all(
        sort_by_owner(raw, owners, prow_count), "prow", split_axis=1, concat_axis=1, tiled=True
    )
    empty = jnp.zeros((2, prow_count, block_size, col_blocks, block_size), jnp.float32)
    placed = place_columns(
        empty,
        lax.all_gather(moved, "pcol", axis=3, tiled=True),
        col_map,
        col_here,
        pcol_count,
        block_size,
    )
    arrived = placed.reshape(2, prow_count, block_size, col_blocks * block_size)
    stacked = matrix.reshape(row_blocks, block_size, col_blocks * block_size)
    for member in range(2):
        stacked = stacked.at[arrival[member]].add(arrived[member])
    matrix = stacked.reshape(row_blocks * block_size, col_blocks * block_size)
    row_ids = (
        (jnp.arange(row_blocks)[:, None] * prow_count + row_here) * block_size
        + jnp.arange(block_size)[None, :]
    ).reshape(-1)
    col_ids = (
        (jnp.arange(col_blocks)[:, None] * pcol_count + col_here) * block_size
        + jnp.arange(block_size)[None, :]
    ).reshape(-1)
    for segment in range(2):
        start_col = 2 * segment * block_size
        stop_col = start_col + 2 * block_size
        strips = [spread(matrix, 2 * segment + member) for member in range(2)]
        panel = jnp.concatenate(strips, axis=1)
        wanted = [jnp.int32(2 * segment), jnp.int32(2 * segment + 1)]
        wanted = wanted + [col_here + 0]
        pieces = []
        for target in wanted:
            section = lax.dynamic_slice_in_dim(
                panel, target // prow_count * block_size, block_size, 0
            )
            pieces.append(jnp.where(target % prow_count == row_here, section, 0.0))
        gathered = lax.psum(jnp.concatenate(pieces, axis=0), "prow")
        diag = gathered[: 2 * block_size]
        sym = jnp.tril(diag) + jnp.tril(diag, -1).T
        lower = jnp.linalg.cholesky(sym)
        inverse = lax.linalg.triangular_solve(
            lower, jnp.eye(2 * block_size, dtype=jnp.float32), left_side=True, lower=True
        )
        factor = jnp.dot(panel, inverse.T, precision=HIGHEST_PRECISION)
        col_factor = jnp.dot(gathered[2 * block_size :], inverse.T, precision=HIGHEST_PRECISION)
        shaped = factor.reshape(row_blocks, block_size, 2 * block_size)
        for member in range(2):
            target = 2 * segment + member
            slot = target // prow_count
            replaced = jnp.where(
                row_here == target % prow_count,
                lower[member * block_size : (member + 1) * block_size],
                shaped[slot],
            )
            shaped = shaped.at[slot].set(replaced)
        factor = shaped.reshape(row_blocks * block_size, 2 * block_size)
        for member in range(2):
            owned = col_here == 2 * segment + member
            written = jnp.where(
                owned, factor[:, member * block_size : (member + 1) * block_size], matrix
            )
            matrix = matrix.at[:, :block_size].set(written)
        change = jnp.dot(factor, col_factor.T, precision=HIGHEST_PRECISION)
        matrix = matrix - jnp.where(col_ids[None, :] >= stop_col, change, 0.0)
    keep = row_ids[:, None] >= jnp.minimum(col_ids, 4 * block_size)[None, :]
    return jnp.where(keep, matrix, 0.0).reshape(front.shape)


def solution(mesh):
    return jax.shard_map(
        on_device,
        mesh=mesh,
        in_specs=(
            P(None, "prow", None, None, "pcol", None),
            P(None, None, "prow", None, "pcol", None),
            P(),
            P(),
        ),
        out_specs=P(None, "prow", None, None, "pcol", None),
        check_vma=False,
    )
```

profile of v0, /device:TPU:0, one launch (start us, length us, event | category | flops | bytes accessed | tf_op | source)
XLA Modules:
  0.0 761.4 jit_solution(10043648452690605606)
XLA Ops:
  6.5 4.5 copy.75
  11.4 1.2 fusion.7
  12.7 20.4 %all_to_all.5 = f32[2,8,128,128]{3,2,0,1:T(8,128)} all-to-all(f32[2,8,128,128]{3,2,0,1:T(8,128)S(1)} %copy.14), channel_id=1, replica_groups=mesh['prow'=8,'pcol'=16] {'prow'}, dimensions={1} | all-to-all | bytes 2097152 | tf_op jit(solution)/shard_map/all_to_all | solution.py:48
  33.2 121.8 %all-gather.2.cloned.1.call-done = f32[2,8,128,2048]{3,2,0,1:T(8,128)} async-done(((f32[2,8,128,128]{3,2,0,1:T(8,128)}), f32[2,8,128,2048]{3,2,0,1:T(8,128)}) %all-gather.2.cloned.1.call-update) | async-done | bytes 16777232 | tf_op jit(solution)/shard_map/all_gather | solution.py:54
  155.0 9.4 %copy.32 = f32[256,8,16,128]{3,2,1,0:T(8,128)S(1)} copy(f32[256,8,16,128]{3,1,2,0:T(8,128)} %bitcast.134) | data formatting | bytes 33554432
  164.4 6.5 fusion
  171.0 2.7 scatter_fusion
  173.7 2.7 scatter_fusion.1
  176.4 5.7 bitcast_select_fusion
  182.2 134.7 %all-reduce.14.cloned.1.call-done = (f32[7552,128]{1,0:T(8,128)}, f32[7552,128]{1,0:T(8,128)}) async-done(((f32[7552,128]{1,0:T(8,128)}, f32[7552,128]{1,0:T(8,128)}), (f32[7552,128]{1,0:T(8,128)}, f32[7552,128]{1,0:T(8,128)})) %all-reduce.14.cloned.1.call-update) | async-done | bytes 7733264 | tf_op jit(solution)/shard_map/psum | solution.py:11
  316.9 2.5 constant_dynamic-update-slice_fusion.1
  319.5 0.7 copy-done.6
  320.2 0.3 constant_dynamic-update-slice_fusion
  320.5 3.0 copy-done.3
  323.6 0.8 pad_maximum_fusion
  324.7 59.9 %all-reduce.8.cloned.1.call-done = f32[384,256]{1,0:T(8,128)} async-done(((f32[384,256]{1,0:T(8,128)}), f32[384,256]{1,0:T(8,128)}) %all-reduce.8.cloned.1.call-update) | async-done | bytes 393232 | tf_op jit(solution)/shard_map/psum | solution.py:86
  384.6 1.0 slice.289
  385.7 1.0 bitcast_add_fusion.3
  387.0 11.7 %cholesky.130 = f32[128,128]{1,0:T(8,128)S(1)} custom-call(f32[128,128]{1,0:T(8,128)S(1)} %cholesky.194), custom_call_target="Cholesky" | custom-call | tf_op jit(solution)/shard_map/jit(cholesky)/cholesky | solution.py:89
  398.7 9.8 %custom-call.13 = f32[1,128,128]{1,2,0:T(8,128)S(1)} custom-call(f32[1,128,128]{2,1,0:T(8,128)S(1)} %get-tuple-element.200), custom_call_target="InvertDiagBlocksLowerTriangular" | custom-call | tf_op jit(solution)/shard_map/jit(cholesky)/cholesky | solution.py:89
  408.8 0.3 convolution_subtract_fusion.3
  409.0 11.7 %cholesky.147 = f32[128,128]{1,0:T(8,128)S(1)} custom-call(f32[128,128]{1,0:T(8,128)S(1)} %convolution_subtract_fusion.3), custom_call_target="Cholesky" | custom-call | tf_op jit(solution)/shard_map/jit(cholesky)/cholesky | solution.py:89
  420.8 0.7 compare_reduce_fusion.2
  422.9 4.3 while.16
  423.1 0.7 fusion.77
  423.8 1.4 bitcast_dynamic-update-slice_fusion.6
  425.2 0.7 fusion.77
  425.8 1.4 bitcast_dynamic-update-slice_fusion.6
  427.2 19.7 %custom-call.14 = f32[2,128,128]{1,2,0:T(8,128)S(1)} custom-call(f32[2,128,128]{2,1,0:T(8,128)S(1)} %get-tuple-element.149), custom_call_target="InvertDiagBlocksLowerTriangular" | custom-call | tf_op jit(solution)/shard_map/triangular_solve/custom-call.0 | solution.py:90
  446.9 0.3 fusion.27
  447.5 0.3 fusion.34
  447.8 9.0 %fusion.18 = f32[7552,256]{1,0:T(8,128)S(1)} fusion(f32[7552,256]{1,0:T(8,128)} %copy-done.3, f32[128,256]{1,0:T(8,128)S(1)} %fusion.34, f32[128,256]{1,0:T(8,128)S(1)} %fusion.27), kind=kOutput, calls=%fused_computation.52 | convolution fusion | flops 5939200000 | bytes 15728640 | tf_op jit(solution)/shard_map/dot_general | solution.py:93
  456.8 0.9 copy.55
  457.7 1.5 fusion.17
  459.2 9.2 %broadcast_select_fusion = (f32[7552,128]{1,0:T(8,128)}, f32[7552,128]{1,0:T(8,128)}, f32[7552,128]{1,0:T(8,128)}) fusion(pred[]{:T(512)S(6)} %eq.100, pred[]{:T(512)S(6)} %eq.101, f32[7552,256]{1,0:T(8,128)S(1)} %bitcast.132, f32[128,256]{1,0:T(8,128)S(1)} %fusion.17, pred[128]{0:T(512)(128)(4,1)S(1)} %fusion.52, f32[7552,128]{1,0:T(8,128)S(1)} %bitcast.131, ...), kind=kOutput, calls=%fused_computation.19 | convolution fusion | flops 2975367168 | bytes 31064580 | tf_op jit(solution)/shard_map/dot_general | solution.py:112
  468.4 0.4 all-reduce.10.cloned.1.call-start
  469.2 134.1 %all-reduce.12.cloned.1.call-done = (f32[7552,128]{1,0:T(8,128)}, f32[7552,128]{1,0:T(8,128)}) async-done(((f32[7552,128]{1,0:T(8,128)}, f32[7552,128]{1,0:T(8,128)}), (f32[7552,128]{1,0:T(8,128)}, f32[7552,128]{1,0:T(8,128)})) %all-reduce.12.cloned.1.call-update) | async-done | bytes 7733264 | tf_op jit(solution)/shard_map/psum | solution.py:11
  603.3 2.5 constant_dynamic-update-slice_fusion.3
  605.8 0.7 copy-done.7
  606.5 0.3 constant_dynamic-update-slice_fusion.2
  606.8 3.0 copy-done.4
  609.9 0.8 pad_maximum_fusion.1
  610.8 60.1 %all-reduce.10.cloned.1.call-done = f32[384,256]{1,0:T(8,128)} async-done(((f32[384,256]{1,0:T(8,128)}), f32[384,256]{1,0:T(8,128)}) %all-reduce.10.cloned.1.call-update) | async-done | bytes 393232 | tf_op jit(solution)/shard_map/psum | solution.py:86
  670.9 1.0 slice_select_fusion.2
  672.0 1.0 bitcast_add_fusion.1
  673.3 11.7 %cholesky.164 = f32[128,128]{1,0:T(8,128)S(1)} custom-call(f32[128,128]{1,0:T(8,128)S(1)} %cholesky.197), custom_call_target="Cholesky" | custom-call | tf_op jit(solution)/shard_map/jit(cholesky)/cholesky | solution.py:89
  685.0 9.8 %custom-call.15 = f32[1,128,128]{1,2,0:T(8,128)S(1)} custom-call(f32[1,128,128]{2,1,0:T(8,128)S(1)} %get-tuple-element.196), custom_call_target="InvertDiagBlocksLowerTriangular" | custom-call | tf_op jit(solution)/shard_map/jit(cholesky)/cholesky | solution.py:89
  695.1 0.3 convolution_subtract_fusion.2
  695.3 11.7 %cholesky.181 = f32[128,128]{1,0:T(8,128)S(1)} custom-call(f32[128,128]{1,0:T(8,128)S(1)} %convolution_subtract_fusion.2), custom_call_target="Cholesky" | custom-call | tf_op jit(solution)/shard_map/jit(cholesky)/cholesky | solution.py:89
  707.1 0.7 compare_reduce_fusion
  707.8 0.6 compare_reduce_fusion.1
  709.9 4.3 while.17
  710.1 0.6 fusion.78
  710.7 1.4 bitcast_dynamic-update-slice_fusion.7
  712.1 0.6 fusion.78
  712.7 1.4 bitcast_dynamic-update-slice_fusion.7
  714.1 19.7 %custom-call.16 = f32[2,128,128]{1,2,0:T(8,128)S(1)} custom-call(f32[2,128,128]{2,1,0:T(8,128)S(1)} %get-tuple-element.150), custom_call_target="InvertDiagBlocksLowerTriangular" | custom-call | tf_op jit(solution)/shard_map/triangular_solve/custom-call.0 | solution.py:90
  733.8 0.3 fusion.25
  734.1 0.3 convolution_subtract_fusion
  734.4 0.3 fusion.30
  734.7 8.5 %fusion.16 = f32[7552,256]{1,0:T(8,128)S(1)} fusion(f32[7552,256]{1,0:T(8,128)} %copy-done.4, f32[128,256]{1,0:T(8,128)S(1)} %fusion.30, f32[128,256]{1,0:T(8,128)S(1)} %fusion.25), kind=kOutput, calls=%fused_computation.50 | convolution fusion | flops 5939200000 | bytes 15728640 | tf_op jit(solution)/shard_map/dot_general | solution.py:93
  743.3 0.9 copy.69
  744.3 1.5 fusion.15
  745.8 8.9 %fusion.4 = f32[7552,128]{1,0:T(8,128)} fusion(f32[7552,256]{1,0:T(8,128)S(1)} %bitcast.133, f32[128,256]{1,0:T(8,128)S(1)} %fusion.15, f32[7552,128]{1,0:T(8,128)S(1)} %copy-done.5, s32[128]{0:T(128)S(1)} %fusion.53, s32[7552]{0:T(1024)S(1)} %add_bitcast_fusion, pred[128]{0:T(512)(128)(4,1)S(1)} %fusion.51, pred[]{:T(512)S(6)} %eq.101, pred[]{:T(512)S(6)} %eq.100), kind=kOutput, calls=%fused_computation.12 | convolution fusion | flops 2975367168 | bytes 23364610 | tf_op jit(solution)/shard_map/dot_general | solution.py:112
  (75 shorter events, 3.1 us)
Async XLA Ops:
  6.5 4.8 copy-start
  6.5 4.6 copy-start.8
  6.5 26.7 %copy-start.9 = (s32[2,16]{1,0:T(2,128)S(1)}, s32[2,16]{1,0:T(2,128)}, u32[]{:S(2)}) copy-start(s32[2,16]{1,0:T(2,128)} %param.34) | copy-start | bytes 388
  6.5 148.5 %all-gather.2.cloned.1.call-start = ((), (), s32[]{:S(2)}) async-start(), calls=%async_computation.1 | async-start | bytes 17825792 | tf_op jit(solution)/shard_map/all_gather | solution.py:54
  33.2 283.8 %all-reduce.14.cloned.1.call-start = ((), (), s32[]{:S(2)}) async-start(), calls=%async_computation.5 | async-start | bytes 15466496 | tf_op jit(solution)/shard_map/psum | solution.py:11
  182.1 202.5 %all-reduce.8.cloned.1.call-start = ((), (), s32[]{:S(2)}) async-start(), calls=%async_computation.2 | async-start | bytes 786432 | tf_op jit(solution)/shard_map/psum | solution.py:86
  316.9 3.3 copy-start.6
  320.5 3.1 copy-start.3
  324.4 278.9 %all-reduce.12.cloned.1.call-start = ((), (), s32[]{:S(2)}) async-start(), calls=%async_computation.4 | async-start | bytes 15466496 | tf_op jit(solution)/shard_map/psum | solution.py:11
  456.8 2.5 copy-start.2
  468.4 202.5 %all-reduce.10.cloned.1.call-start = ((), (), s32[]{:S(2)}) async-start(), calls=%async_computation.3 | async-start | bytes 786432 | tf_op jit(solution)/shard_map/psum | solution.py:86
  603.3 3.3 copy-start.7
  606.8 3.1 copy-start.4
  743.3 2.5 copy-start.5
  745.7 9.0 %copy-start.1 = (f32[2,8,1,128,1,128]{5,4,3,2,1,0:T(1,128)S(1)}, f32[2,8,1,128,1,128]{5,4,3,2,1,0:T(1,128)}, u32[]{:S(2)}) copy-start(f32[2,8,1,128,1,128]{5,4,3,2,1,0:T(1,128)} %param.32) | copy-start | bytes 3145732
Sparse Core Ops, SparseCore 0:
  33.3 121.7 all-gather.1
  182.2 134.6 all-reduce.13
  324.5 60.0 all-reduce.7
  468.6 134.6 all-reduce.11
  610.8 60.0 all-reduce.9
where the time goes:
time: 769 us; the launch traced here: 761 us
  waiting for transfers between devices  511 us (66%)
  other arithmetic  124 us (16%)
  matrix products  49 us (6%)
  local copies, waits for them, and re-layouts  39.2 us (5%)
  blocking collectives  20.4 us (3%)
  between operations  16.6 us (2%)
    psum x2, waiting for transfers between devices, broadcast(): return lax.psum(block, axis)  269 us
    all_gather x1, waiting for transfers between devices, on_device(): lax.all_gather(moved, 'pcol', axis=3, tiled=True)  122 us
    psum x2, waiting for transfers between devices, on_device(): gathered = lax.psum(jnp.concatenate(pieces, axis=0), 'prow')  120 us
    another operation x13, other arithmetic, on_device(): lower = jnp.linalg.cholesky(sym)  68.7 us
    another operation x5, other arithmetic, on_device(): lax.linalg.triangular_solve(lower, jnp.eye(2 * block_size, dtype=jnp.floa...  39.4 us
    unnamed x26, local copies, waits for them, and re-layouts  28.4 us
    all_to_all x1, blocking collectives, on_device(): lax.all_to_all(sort_by_owner(raw, owners, prow_count), 'prow', split_axis...  20.4 us
    dot_general x2, matrix products, on_device(): change = jnp.dot(factor, col_factor.T, precision=HIGHEST_PRECISION)  18.1 us
  transfers between devices with their start and end apart: 5, of which 5 were waited for; matrix products, arithmetic and copies ran while one was open for 0% of the time, Pallas kernels for 0%

commit v1 on v0

--- a/solution.py
+++ b/solution.py
@@ -49,13 +49,11 @@
         sort_by_owner(raw, owners, prow_count), "prow", split_axis=1, concat_axis=1, tiled=True
     )
     empty = jnp.zeros((2, prow_count, block_size, col_blocks, block_size), jnp.float32)
+    connect_slices = lambda state, net_axis: jnp.concatenate(
+        lax.all_to_all(jnp.stack([state for _ in range(lax.psum(1, net_axis))]), net_axis, 0, 0), 3
+    )
     placed = place_columns(
-        empty,
-        lax.all_gather(moved, "pcol", axis=3, tiled=True),
-        col_map,
-        col_here,
-        pcol_count,
-        block_size,
+        empty, connect_slices(moved, "pcol"), col_map, col_here, pcol_count, block_size
     )
     arrived = placed.reshape(2, prow_count, block_size, col_blocks * block_size)
     stacked = matrix.reshape(row_blocks, block_size, col_blocks * block_size)

time: 769 us -> 961 us (1.25)
  waiting for transfers between devices: 511 us -> 686 us
  matrix products: 49 us -> 63.1 us
    all_to_all x0 -> x1, waiting for transfers between devices: none -> 291 us  [on_device(): lax.all_to_all(jnp.stack([state for _ in range(lax.psum(1, net_axis))]),...]
    all_gather x1 -> x0, waiting for transfers between devices: 122 us -> none  [on_device(): lax.all_gather(moved, 'pcol', axis=3, tiled=True)]
    dot_general x1, matrix products: 6.49 us -> 20.6 us  [place_columns(): jnp.einsum('csrtk,ctm->csrmk', shaped, pick, precision=HIGHEST_PRECISION)]
    unnamed x26 -> x25, local copies, waits for them, and re-layouts: 28.4 us -> 19 us
where the time goes in v1:
time: 961 us; the launch traced here: 958 us
  waiting for transfers between devices  686 us (71%)
  other arithmetic  124 us (13%)
  matrix products  63.1 us (7%)
  local copies, waits for them, and re-layouts  37.4 us (4%)
  blocking collectives  20.3 us (2%)
  between operations  16.5 us (2%)
    all_to_all x1, waiting for transfers between devices, on_device(): lax.all_to_all(jnp.stack([state for _ in range(lax.psum(1, net_axis))]),...  291 us
    psum x2, waiting for transfers between devices, broadcast(): return lax.psum(block, axis)  275 us
    psum x2, waiting for transfers between devices, on_device(): gathered = lax.psum(jnp.concatenate(pieces, axis=0), 'prow')  120 us
    another operation x13, other arithmetic, on_device(): lower = jnp.linalg.cholesky(sym)  68.6 us
    another operation x5, other arithmetic, on_device(): lax.linalg.triangular_solve(lower, jnp.eye(2 * block_size, dtype=jnp.floa...  39.4 us
    dot_general x1, matrix products, place_columns(): jnp.einsum('csrtk,ctm->csrmk', shaped, pick, precision=HIGHEST_PRECISION)  20.6 us
    all_to_all x1, blocking collectives, on_device(): lax.all_to_all(sort_by_owner(raw, owners, prow_count), 'prow', split_axis...  20.3 us
  transfers between devices with their start and end apart: 5, of which 5 were waited for; matrix products, arithmetic and copies ran while one was open for 0% of the time, Pallas kernels for 0%

profile of v1, /device:TPU:0, one launch (start us, length us, event | category | flops | bytes accessed | tf_op | source)
XLA Modules:
  0.0 957.6 jit_solution(15405921732672675661)
XLA Ops:
  6.5 4.6 copy.74
  11.4 1.2 fusion.7
  12.7 20.3 %all_to_all.10 = f32[2,8,128,128]{3,2,0,1:T(8,128)S(1)} all-to-all(f32[2,8,128,128]{3,2,0,1:T(8,128)S(1)} %copy.22), channel_id=1, replica_groups=mesh['prow'=8,'pcol'=16] {'prow'}, dimensions={1} | all-to-all | bytes 2097152 | tf_op jit(solution)/shard_map/all_to_all | solution.py:48
  33.1 7.8 stack.2
  41.0 8.2 all-to-all-start.1
  49.5 291.1 %all-to-all-done.1 = f32[16,2,8,128,128]{4,3,2,1,0:T(8,128)} async-done(((f32[16,2,8,128,128]{4,3,2,1,0:T(8,128)}), f32[16,2,8,128,128]{4,3,2,1,0:T(8,128)}, u32[]{:S(2)}, u32[]{:S(2)}) %all-to-all-start.1) | async-done | bytes 16777248 | tf_op jit(solution)/shard_map/all_to_all | solution.py:53
  340.5 20.6 %fusion = f32[2,1,8,128,128]{4,1,3,2,0:T(1,128)S(1)} fusion(f32[2,8,128,16,128]{4,2,1,0,3:T(8,128)} %bitcast.8, pred[2,16,1,1,1]{1,0,2,3,4:T(4,128)(4,1)S(1)} %compare_bitcast_fusion), kind=kOutput, calls=%fused_computation.6 | convolution fusion | flops 50331648 | bytes 17825824 | tf_op jit(solution)/shard_map/csrtk,ctm->csrmk/dot_general | solution.py:28
  361.2 2.7 scatter_fusion
  363.9 2.7 scatter_fusion.1
  366.6 5.7 bitcast_select_fusion
  372.5 140.8 %all-reduce.14.cloned.1.call-done = (f32[7552,128]{1,0:T(8,128)}, f32[7552,128]{1,0:T(8,128)}) async-done(((f32[7552,128]{1,0:T(8,128)}, f32[7552,128]{1,0:T(8,128)}), (f32[7552,128]{1,0:T(8,128)}, f32[7552,128]{1,0:T(8,128)})) %all-reduce.14.cloned.1.call-update) | async-done | bytes 7733264 | tf_op jit(solution)/shard_map/psum | solution.py:11
  513.3 2.5 constant_dynamic-update-slice_fusion.1
  515.8 0.7 copy-done.6
  516.5 0.3 constant_dynamic-update-slice_fusion
  516.9 3.0 copy-done.3
  519.9 0.8 pad_maximum_fusion
  521.1 59.9 %all-reduce.8.cloned.1.call-done = f32[384,256]{1,0:T(8,128)} async-done(((f32[384,256]{1,0:T(8,128)}), f32[384,256]{1,0:T(8,128)}) %all-reduce.8.cloned.1.call-update) | async-done | bytes 393232 | tf_op jit(solution)/shard_map/psum | solution.py:84
  581.0 1.0 slice.289
  582.1 1.0 bitcast_add_fusion.3
  583.3 11.7 %cholesky.130 = f32[128,128]{1,0:T(8,128)S(1)} custom-call(f32[128,128]{1,0:T(8,128)S(1)} %cholesky.194), custom_call_target="Cholesky" | custom-call | tf_op jit(solution)/shard_map/jit(cholesky)/cholesky | solution.py:87
  595.1 9.8 %custom-call.13 = f32[1,128,128]{1,2,0:T(8,128)S(1)} custom-call(f32[1,128,128]{2,1,0:T(8,128)S(1)} %get-tuple-element.200), custom_call_target="InvertDiagBlocksLowerTriangular" | custom-call | tf_op jit(solution)/shard_map/jit(cholesky)/cholesky | solution.py:87
  605.1 0.3 convolution_subtract_fusion.3
  605.4 11.7 %cholesky.147 = f32[128,128]{1,0:T(8,128)S(1)} custom-call(f32[128,128]{1,0:T(8,128)S(1)} %convolution_subtract_fusion.3), custom_call_target="Cholesky" | custom-call | tf_op jit(solution)/shard_map/jit(cholesky)/cholesky | solution.py:87
  617.2 0.7 compare_reduce_fusion.2
  619.2 4.3 while.16
  619.7 0.6 fusion.77
  620.3 1.3 bitcast_dynamic-update-slice_fusion.6
  621.6 0.6 fusion.77
  622.2 1.3 bitcast_dynamic-update-slice_fusion.6
  623.5 19.7 %custom-call.14 = f32[2,128,128]{1,2,0:T(8,128)S(1)} custom-call(f32[2,128,128]{2,1,0:T(8,128)S(1)} %get-tuple-element.149), custom_call_target="InvertDiagBlocksLowerTriangular" | custom-call | tf_op jit(solution)/shard_map/triangular_solve/custom-call.0 | solution.py:88
  643.2 0.3 fusion.27
  643.5 0.3 convolution_subtract_fusion.1
  643.8 0.3 fusion.34
  644.1 9.0 fusion.18
  653.1 0.9 copy.54
  654.1 1.5 fusion.17
  655.6 9.2 broadcast_select_fusion
  665.3 134.3 %all-reduce.12.cloned.1.call-done = (f32[7552,128]{1,0:T(8,128)}, f32[7552,128]{1,0:T(8,128)}) async-done(((f32[7552,128]{1,0:T(8,128)}, f32[7552,128]{1,0:T(8,128)}), (f32[7552,128]{1,0:T(8,128)}, f32[7552,128]{1,0:T(8,128)})) %all-reduce.12.cloned.1.call-update) | async-done | bytes 7733264 | tf_op jit(solution)/shard_map/psum | solution.py:11
  799.6 2.5 constant_dynamic-update-slice_fusion.3
  802.1 0.7 copy-done.7
  802.8 0.3 constant_dynamic-update-slice_fusion.2
  803.2 3.0 copy-done.4
  806.2 0.8 pad_maximum_fusion.1
  807.1 60.1 %all-reduce.10.cloned.1.call-done = f32[384,256]{1,0:T(8,128)} async-done(((f32[384,256]{1,0:T(8,128)}), f32[384,256]{1,0:T(8,128)}) %all-reduce.10.cloned.1.call-update) | async-done | bytes 393232 | tf_op jit(solution)/shard_map/psum | solution.py:84
  867.2 1.0 slice_select_fusion.2
  868.3 1.0 bitcast_add_fusion.1
  869.6 11.7 %cholesky.164 = f32[128,128]{1,0:T(8,128)S(1)} custom-call(f32[128,128]{1,0:T(8,128)S(1)} %cholesky.197), custom_call_target="Cholesky" | custom-call | tf_op jit(solution)/shard_map/jit(cholesky)/cholesky | solution.py:87
  881.4 9.8 %custom-call.15 = f32[1,128,128]{1,2,0:T(8,128)S(1)} custom-call(f32[1,128,128]{2,1,0:T(8,128)S(1)} %get-tuple-element.196), custom_call_target="InvertDiagBlocksLowerTriangular" | custom-call | tf_op jit(solution)/shard_map/jit(cholesky)/cholesky | solution.py:87
  891.4 0.3 convolution_subtract_fusion.2
  891.7 11.7 %cholesky.181 = f32[128,128]{1,0:T(8,128)S(1)} custom-call(f32[128,128]{1,0:T(8,128)S(1)} %convolution_subtract_fusion.2), custom_call_target="Cholesky" | custom-call | tf_op jit(solution)/shard_map/jit(cholesky)/cholesky | solution.py:87
  903.4 0.7 compare_reduce_fusion
  904.1 0.6 compare_reduce_fusion.1
  906.1 4.2 while.17
  906.3 0.6 fusion.78
  906.9 1.4 bitcast_dynamic-update-slice_fusion.7
  908.3 0.6 fusion.78
  908.9 1.4 bitcast_dynamic-update-slice_fusion.7
  910.3 19.7 %custom-call.16 = f32[2,128,128]{1,2,0:T(8,128)S(1)} custom-call(f32[2,128,128]{2,1,0:T(8,128)S(1)} %get-tuple-element.150), custom_call_target="InvertDiagBlocksLowerTriangular" | custom-call | tf_op jit(solution)/shard_map/triangular_solve/custom-call.0 | solution.py:88
  929.9 0.3 fusion.25
  930.5 0.3 fusion.30
  930.9 8.6 fusion.16
  939.4 0.9 copy.68
  940.4 1.5 fusion.15
  941.9 8.9 fusion.4
  (75 shorter events, 3.6 us)
Async XLA Ops:
  6.5 4.8 copy-start
  6.5 4.6 copy-start.8
  41.0 8.5 copy-start.9
  41.0 299.6 %all-to-all-start.1 = ((f32[16,2,8,128,128]{4,3,2,1,0:T(8,128)}), f32[16,2,8,128,128]{4,3,2,1,0:T(8,128)}, u32[]{:S(2)}, u32[]{:S(2)}) async-start(f32[16,2,8,128,128]{4,3,2,1,0:T(8,128)} %stack.2), calls=%async_computation.1 | async-start | bytes 33554432 | tf_op jit(solution)/shard_map/all_to_all | solution.py:53
  49.2 464.1 %all-reduce.14.cloned.1.call-start = ((), (), s32[]{:S(2)}) async-start(), calls=%async_computation.5 | async-start | bytes 15466496 | tf_op jit(solution)/shard_map/psum | solution.py:11
  372.4 208.6 %all-reduce.8.cloned.1.call-start = ((), (), s32[]{:S(2)}) async-start(), calls=%async_computation.2 | async-start | bytes 786432 | tf_op jit(solution)/shard_map/psum | solution.py:84
  513.3 3.3 copy-start.6
  516.9 3.1 copy-start.3
  520.8 278.8 %all-reduce.12.cloned.1.call-start = ((), (), s32[]{:S(2)}) async-start(), calls=%async_computation.4 | async-start | bytes 15466496 | tf_op jit(solution)/shard_map/psum | solution.py:11
  653.1 2.5 copy-start.2
  664.8 202.4 %all-reduce.10.cloned.1.call-start = ((), (), s32[]{:S(2)}) async-start(), calls=%async_computation.3 | async-start | bytes 786432 | tf_op jit(solution)/shard_map/psum | solution.py:84
  799.6 3.3 copy-start.7
  803.2 3.1 copy-start.4
  939.4 2.5 copy-start.5
  941.9 9.0 copy-start.1
Sparse Core Ops, SparseCore 0:
  372.5 140.7 all-reduce.13
  520.9 60.0 all-reduce.7
  664.9 134.6 all-reduce.11
  807.2 60.0 all-reduce.9
